TPU v7x, 32 devices: a whole 2x2x4 slice. The times are simulated.
32 devices in a mesh: tr: 8 (over z, x), tc: 4 (over y, core).
Axes of the slice: x: 2, y: 2, z: 4, core: 2. Of those that a mesh axis runs over, the one named last changes fastest.
Arguments:
- design: float32 [1024, 16384], P('tr', 'tc'), may hold values from -0.1875 to 0.1875
- taps: float32 [128], replicated, may hold values from -0.5 to 0.5
- order: int32 [16384], replicated, may hold values from 0 to 16383, each once
- normal_in: float32 [16384, 16384], P('tr', 'tc'), may hold values from -6 to 6
Outputs:
- normal_out: float32 [16384, 16384], P('tr', 'tc')
Inputs may be any that keep to these rules, and one draw needn't show every extreme that they name: order is a permutation: every design column appears exactly once.
All inputs are finite; a program needn't handle non-finite values.
Results may differ from a plain program's by a relative error of at most 0.00005.
Values sent between devices are 32-bit elements; how exact they have to be, the bound alone decides.
A program may use at most 192 MiB of HBM per device.

v0:
```python
import jax
import jax.numpy as jnp
from jax import lax
from jax.sharding import PartitionSpec as P


def shifted(shard, axis, by):
    count = lax.axis_size(axis)
    pairs = [(i, i + by) for i in range(count) if 0 <= i + by < count]
    return lax.ppermute(shard, axis, pairs)


def contract_rows(left_rows, right_rows):
    return lax.dot_general(
        left_rows,
        right_rows,
        (((1,), (1,)), ((), ())),
        precision=lax.Precision.HIGHEST,
        preferred_element_type=jnp.float32,
    )


def body(design, taps, order, normal_in):
    row_count, col_count = design.shape
    tap_count = taps.shape[0]
    tail_rows = design[row_count - (tap_count - 1) :]
    before = shifted(tail_rows, "tr", 1)
    extended = jnp.concatenate([before, design], axis=0)
    time_index = jnp.arange(row_count, dtype=jnp.int32)[:, None]
    source_index = jnp.arange(row_count + tap_count - 1, dtype=jnp.int32)[None, :]
    lag_index = time_index + (tap_count - 1) - source_index
    inside = (lag_index >= 0) & (lag_index < tap_count)
    toeplitz = jnp.where(inside, jnp.take(taps, jnp.clip(lag_index, 0, tap_count - 1)), 0.0)
    filtered_cols = lax.dot_general(
        extended,
        toeplitz,
        (((0,), (1,)), ((), ())),
        precision=lax.Precision.HIGHEST,
        preferred_element_type=jnp.float32,
    )
    full_width = lax.all_gather(filtered_cols, "tc", axis=0, tiled=True)
    ordered = jnp.take(full_width, order, axis=0)
    width_rows = ordered.shape[0] // lax.axis_size("tr")
    width_cols = ordered.shape[0] // lax.axis_size("tc")
    row_start = lax.axis_index("tr") * width_rows
    col_start = lax.axis_index("tc") * width_cols
    block_rows = lax.all_to_all(ordered, "tr", split_axis=0, concat_axis=1, tiled=True)
    col_piece = lax.dynamic_slice_in_dim(ordered, col_start, width_cols, 0)
    active = row_start + width_rows - 1 >= col_start
    empty_tile = jnp.zeros((width_rows, width_cols), jnp.float32)
    col_all = lax.all_gather(col_piece, "tr", axis=1, tiled=True)
    gram = lax.cond(active, lambda: contract_rows(block_rows, col_all), lambda: empty_tile)
    global_rows = row_start + jnp.arange(width_rows, dtype=jnp.int32)[:, None]
    global_cols = col_start + jnp.arange(width_cols, dtype=jnp.int32)[None, :]
    return normal_in + jnp.where(global_rows >= global_cols, gram, 0.0)


def solution(mesh):
    return jax.shard_map(
        body,
        mesh=mesh,
        in_specs=(P("tr", "tc"), P(), P(), P("tr", "tc")),
        out_specs=P("tr", "tc"),
        check_vma=False,
    )
```

profile of v0, /device:TPU:24, one launch (start us, length us, event | category | flops | bytes accessed | tf_op | source)
XLA Modules:
  0.0 872.1 jit_solution(1333697999465449814)
XLA Ops:
  6.5 0.0 copy-start
  6.5 0.0 all-gather.3.cloned.1.call-start
  6.5 3.1 slice.3
  9.6 3.4 collective-permute-start
  13.0 0.1 compare_select_fusion
  13.2 0.3 reshape.91
  13.5 0.0 copy-done
  13.5 0.0 copy-start.2
  13.5 181.1 %gather_fusion = f32[32640]{0:T(1024)S(1)} fusion(f32[128]{0:T(128)S(1)} %copy-done, s32[32768]{0:T(1024)S(1)} %pad_clamp_fusion), kind=kCustom, calls=%fused_computation | custom fusion | bytes 391680 | tf_op jit(solution)/shard_map/jit(_take)/gather | solution.py:33
  194.7 0.0 copy-start.3
  194.7 0.3 reshape.90
  195.0 0.0 collective-permute-done
  195.0 0.0 copy-done.2
  195.0 9.7 %fusion.3 = f32[4096,128]{1,0:T(8,128)} fusion(f32[128,4096]{1,0:T(8,128)S(1)} %copy-done.2, f32[127,4096]{1,0:T(8,128)} %collective-permute-done, f32[128,255]{1,0:T(8,128)S(1)} %reshape.90, s32[128]{0:T(128)S(1)} %iota_add_fusion.2), kind=kOutput, calls=%fused_computation.6 | convolution fusion | flops 1605790080 | bytes 6406144 | tf_op jit(solution)/shard_map/dot_general | solution.py:34
  204.8 0.0 all-gather.3.cloned.1.call-update
  204.8 0.0 all-gather.5.cloned.1.call-start
  204.9 0.0 copy-done.3
  204.9 58.4 %all-gather.3.cloned.1.call-done = f32[16384,128]{1,0:T(8,128)} async-done(((f32[4096,128]{1,0:T(8,128)}), f32[16384,128]{1,0:T(8,128)}) %all-gather.3.cloned.1.call-update) | async-done | bytes 8388624 | tf_op jit(solution)/shard_map/all_gather | solution.py:41
  263.3 58.2 %gather_fusion.1 = f32[16384,128]{1,0:T(8,128)} fusion(f32[16384,128]{1,0:T(8,128)} %all-gather.3.cloned.1.call-done, s32[16384]{0:T(1024)S(1)} %fusion.24), kind=kCustom, calls=%fused_computation.1 | custom fusion | bytes 16842752 | tf_op jit(solution)/shard_map/jit(_take)/gather | solution.py:42
  321.5 4.7 dynamic-slice_select_fusion
  326.2 0.0 all-gather.5.cloned.1.call-update
  326.3 10.1 %broadcast_select_fusion = f32[8,2048,128]{2,1,0:T(8,128)} fusion(f32[8,2048,128]{2,1,0:T(8,128)} %bitcast.17, pred[8,2048]{1,0:T(8,128)(4,1)S(1)} %broadcast_in_dim.39), kind=kLoop, calls=%fused_computation.10 | loop fusion | flops 2097152 | bytes 16793600 | tf_op jit(solution)/shard_map/jit(_take)/select_n | solution.py:42
  336.4 6.0 all-to-all-start
  342.4 315.3 %all-to-all-done = f32[8,2048,128]{2,1,0:T(8,128)} async-done(((f32[8,2048,128]{2,1,0:T(8,128)}), f32[8,2048,128]{2,1,0:T(8,128)}, u32[]{:S(2)}, u32[]{:S(2)}) %all-to-all-start) | async-done | bytes 8388640 | tf_op jit(solution)/shard_map/all_to_all | solution.py:47
  657.7 63.3 %all-gather.5.cloned.1.call-done = f32[4096,1024]{1,0:T(8,128)} async-done(((f32[4096,128]{1,0:T(8,128)}), f32[4096,1024]{1,0:T(8,128)}) %all-gather.5.cloned.1.call-update) | async-done | bytes 16777232 | tf_op jit(solution)/shard_map/all_gather | solution.py:51
  721.0 111.7 %conditional.1 = (f32[2048,4096]{1,0:T(8,128)}) conditional(s32[]{:T(128)} %convert_element_type.3, () %tuple.11, (f32[2048,8,128]{2,0,1:T(8,128)}, f32[4096,1024]{1,0:T(8,128)}) %tuple.12), branch_computations={%region_0.1_spmd, %region_1.2_spmd} | conditional | flops 103079215104 | bytes 58720264 | solution.py:52
  721.0 111.7 %fusion = f32[2048,4096]{1,0:T(8,128)} fusion(f32[4096,1024]{1,0:T(8,128)} %get-tuple-element.14, f32[2048,8,128]{2,0,1:T(8,128)} %get-tuple-element.15), kind=kOutput, calls=%fused_computation.2 | convolution fusion | flops 103079215104 | bytes 58720256 | tf_op jit(solution)/shard_map/cond/branch_1_fun/dot_general | solution.py:14
  832.8 0.0 copy-start.1
  832.8 32.5 %select_add_fusion = f32[2048,4096]{1,0:T(8,128)} fusion(f32[2048,4096]{1,0:T(8,128)} %param.9, f32[2048,4096]{1,0:T(8,128)} %get-tuple-element.17, s32[4096]{0:T(1024)S(1)} %iota_add_fusion, s32[2048]{0:T(1024)S(1)} %iota_add_fusion.1), kind=kLoop, calls=%fused_computation.5 | loop fusion | flops 25165824 | bytes 100687872 | tf_op jit(solution)/shard_map/add | solution.py:55
  865.2 0.0 copy-done.1
  (8 shorter events, 0.1 us)
Async XLA Ops:
  6.5 7.0 copy-start
  6.5 256.8 %all-gather.3.cloned.1.call-start = ((), (), s32[]{:S(2)}) async-start(), calls=%async_computation.1 | async-start | bytes 10485760 | tf_op jit(solution)/shard_map/all_gather | solution.py:41
  9.6 185.4 %collective-permute-start = (f32[127,4096]{1,0:T(8,128)}, f32[127,4096]{1,0:T(8,128)}, u32[]{:S(2)}, u32[]{:S(2)}) collective-permute-start(f32[127,4096]{1,0:T(8,128)} %slice.3), channel_id=1, source_target_pairs={{0,4},{4,8},{8,12},{12,16},{16,20},{20,24},{24,28},{1,5},{5,9},{9,... | collective-permute-start | bytes 6242312 | tf_op jit(solution)/shard_map/ppermute | solution.py:10
  13.5 181.5 %copy-start.2 = (f32[128,4096]{1,0:T(8,128)S(1)}, f32[128,4096]{1,0:T(8,128)}, u32[]{:S(2)}) copy-start(f32[128,4096]{1,0:T(8,128)} %param.6) | copy-start | bytes 6291460
  194.7 10.2 %copy-start.3 = (s32[16384]{0:T(1024)S(1)}, s32[16384]{0:T(1024)}, u32[]{:S(2)}) copy-start(s32[16384]{0:T(1024)} %param.8) | copy-start | bytes 196612
  204.8 516.2 %all-gather.5.cloned.1.call-start = ((), (), s32[]{:S(2)}) async-start(), calls=%async_computation.2 | async-start | bytes 18874368 | tf_op jit(solution)/shard_map/all_gather | solution.py:51
  336.4 321.3 %all-to-all-start = ((f32[8,2048,128]{2,1,0:T(8,128)}), f32[8,2048,128]{2,1,0:T(8,128)}, u32[]{:S(2)}, u32[]{:S(2)}) async-start(f32[8,2048,128]{2,1,0:T(8,128)} %broadcast_select_fusion), calls=%async_computation | async-start | bytes 16777216 | tf_op jit(solution)/shard_map/all_to_all | solution.py:47
  832.8 32.5 %copy-start.1 = (f32[128]{0:T(128)S(1)}, f32[128]{0:T(128)}, u32[]{:S(2)}) copy-start(f32[128]{0:T(128)} %param.7) | copy-start | bytes 1540
Sparse Core Ops, SparseCore 0:
  204.9 58.3 all-gather.2
  326.4 394.6 all-gather.4
where the time goes:
time: 878 us; the launch traced here: 872 us
  waiting for transfers between devices  437 us (50%)
  local copies, waits for them, and re-layouts  243 us (28%)
  matrix products  121 us (14%)
  other arithmetic  47.5 us (5%)
  between operations  13.5 us (2%)
  starting transfers between devices  9.44 us (1%)
    all_to_all x1, waiting for transfers between devices, body(): lax.all_to_all(ordered, 'tr', split_axis=0, concat_axis=1, tiled=True)  315 us
    gather x2, local copies, waits for them, and re-layouts, body(): jnp.take(taps, jnp.clip(lag_index, 0, tap_count - 1))  181 us
    dot_general x1, matrix products, contract_rows(): lax.dot_general(left_rows, right_rows, (((1,), (1,)), ((), ())), precisio...  112 us
    all_gather x1, waiting for transfers between devices, body(): col_all = lax.all_gather(col_piece, 'tr', axis=1, tiled=True)  63.3 us
    all_gather x1, waiting for transfers between devices, body(): full_width = lax.all_gather(filtered_cols, 'tc', axis=0, tiled=True)  58.4 us
    gather x1, local copies, waits for them, and re-layouts, body(): ordered = jnp.take(full_width, order, axis=0)  58.2 us
    add x1, other arithmetic, body(): return normal_in + jnp.where(global_rows >= global_cols, gram, 0.0)  32.5 us
  transfers between devices with their start and end apart: 4, of which 3 were waited for; matrix products, arithmetic and copies ran while one was open for 22% of the time, Pallas kernels for 0%

commit v1 on v0

v1 whole, which is shorter than its diff:
```python
import functools

import jax
import jax.numpy as jnp
from jax import lax
from jax.experimental import pallas as pl
from jax.experimental.pallas import tpu as pltpu
from jax.sharding import PartitionSpec as P

MESH = pl.DeviceIdType.MESH
VMEM_LIMIT = 56 * 1024 * 1024


def tile_of(extent, most):
    while extent % most:
        most //= 2
    return most


def toeplitz_of(taps, rows):
    count = taps.shape[0]
    line = jnp.concatenate([jnp.zeros((rows,), taps.dtype), taps, jnp.zeros((2 * rows + 1 - count,), taps.dtype)])
    length = line.shape[0]
    skewed = jnp.tile(line, 2 * rows)[: 2 * rows * (length - 1)].reshape(2 * rows, length - 1)
    return skewed[:, 2 * rows : 3 * rows]


def split(value):
    high = value.astype(jnp.bfloat16)
    return high, (value - high.astype(jnp.float32)).astype(jnp.bfloat16)


def permute_kernel(order_ref, src_ref, out_ref):
    count = out_ref.shape[0]
    unroll = 16

    def step(block, carry):
        base = pl.multiple_of(block * unroll, unroll)
        for lane in range(unroll):
            out_ref[pl.ds(base + lane, 1), :] = src_ref[pl.ds(order_ref[base + lane], 1), :]
        return carry

    lax.fori_loop(0, count // unroll, step, 0)


def permute_rows(source, order):
    count, width = order.shape[0], source.shape[1]
    return pl.pallas_call(
        permute_kernel,
        grid_spec=pltpu.PrefetchScalarGridSpec(
            num_scalar_prefetch=1,
            grid=(1,),
            in_specs=[pl.BlockSpec(source.shape, lambda i, o: (0, 0))],
            out_specs=pl.BlockSpec((count, width), lambda i, o: (0, 0)),
        ),
        out_shape=jax.ShapeDtypeStruct((count, width), jnp.float32),
        compiler_params=pltpu.CompilerParams(vmem_limit_bytes=VMEM_LIMIT),
    )(order, source)


def ring_next(index, count):
    even = lax.rem(index, 2) == 0
    up = jnp.where(index + 2 < count, index + 2, index + 1)
    down = jnp.where(index >= 2, index - 2, 0)
    return jnp.where(even, up, down)


def ring_place(index, count):
    half = lax.div(index, 2)
    return jnp.where(lax.rem(index, 2) == 0, half, count - 1 - half)


def ring_member(place, count):
    place = lax.rem(place + 2 * count, count)
    return jnp.where(place < count // 2, 2 * place, 2 * (count - 1 - place) + 1)


def spread_kernel(count, lanes, wide, tall, piece_ref, out_ref, own_sem, rs_sem, rr_sem, ls_sem, lr_sem, cs_sem, cr_sem, fill_sem):
    row = lax.axis_index("tr")
    col = lax.axis_index("tc")
    place = ring_place(row, count)
    right = ring_member(place + 1, count)
    left = ring_member(place - 1, count)
    owner = lax.div(row * tall, wide)
    offset = pl.multiple_of(lax.rem(row * tall, wide), tall)

    barrier = pltpu.get_barrier_semaphore()
    for near in (left, right):
        pl.semaphore_signal(barrier, inc=1, device_id=(near, col), device_id_type=MESH)

    @pl.when(col > 0)
    def _():
        pl.semaphore_signal(barrier, inc=1, device_id=(row, col - 1), device_id_type=MESH)

    @pl.when(col < lanes - 1)
    def _():
        pl.semaphore_signal(barrier, inc=1, device_id=(row, col + 1), device_id_type=MESH)

    peers = 2 + (col > 0).astype(jnp.int32) + (col < lanes - 1).astype(jnp.int32)
    pl.semaphore_wait(barrier, peers)

    own = pltpu.make_async_copy(piece_ref, out_ref.at[row, pl.ds(0, wide)], own_sem)
    own.start()

    steps = count // 2

    def ring(step, sign):
        slot = ring_member(place - sign * step, count)
        last = step == steps - 1
        begin, size = (0, wide)
        if last:
            begin, size = (0 if sign > 0 else wide // 2, wide // 2)
        rows = pl.ds(begin, size)
        source = piece_ref.at[rows] if step == 0 else out_ref.at[slot, rows]
        send, recv = (rs_sem, rr_sem) if sign > 0 else (ls_sem, lr_sem)
        return pltpu.make_async_remote_copy(
            src_ref=source,
            dst_ref=out_ref.at[slot, rows],
            send_sem=send.at[step],
            recv_sem=recv.at[step],
            device_id=(right if sign > 0 else left, col),
            device_id_type=MESH,
        )

    def chain(turn, slot, from_piece):
        if from_piece:
            source = piece_ref.at[pl.ds(offset, tall)]
        else:
            source = out_ref.at[slot, pl.ds(offset, tall)]
        target = out_ref.at[slot, pl.ds(wide, tall)]
        first = pltpu.make_async_remote_copy(
            src_ref=source, dst_ref=target, send_sem=cs_sem.at[turn], recv_sem=cr_sem.at[turn],
            device_id=(row, col - 1), device_id_type=MESH,
        )
        relay = pltpu.make_async_remote_copy(
            src_ref=target, dst_ref=target, send_sem=cs_sem.at[turn], recv_sem=cr_sem.at[turn],
            device_id=(row, col - 1), device_id_type=MESH,
        )
        fill = pltpu.make_async_copy(source, target, fill_sem.at[turn])
        return first, relay, fill

    offsets = [[0]] + [[-s, s] for s in range(1, steps)] + [[steps]]
    turns = []
    for group in offsets:
        turns.append([(len(sum(turns, [])) + i, off) for i, off in enumerate(group)])

    def chain_owner(level):
        for turn, off in turns[level]:
            first, _, fill = chain(turn, ring_member(place + off, count), level == 0)

            @pl.when(col == owner)
            def _():
                fill.start()

            @pl.when((col == owner) & (col > 0))
            def _():
                first.start()

    def chain_relay(level):
        for turn, off in turns[level]:
            _, relay, _ = chain(turn, ring_member(place + off, count), level == 0)

            @pl.when(col < owner)
            def _():
                relay.wait_recv()

            @pl.when((col < owner) & (col > 0))
            def _():
                relay.start()

    for step in range(steps):
        ring(step, 1).start()
        ring(step, -1).start()
        chain_owner(step)
        if step >= 1:
            chain_relay(step - 1)
        ring(step, 1).wait_recv()
        ring(step, -1).wait_recv()
    chain_owner(steps)
    chain_relay(steps - 1)
    chain_relay(steps)

    own.wait()
    for step in range(steps):
        ring(step, 1).wait_send()
        ring(step, -1).wait_send()
    for level in range(steps + 1):
        for turn, off in turns[level]:
            first, _, fill = chain(turn, ring_member(place + off, count), level == 0)

            @pl.when(col == owner)
            def _():
                fill.wait()

            @pl.when((col <= owner) & (col > 0))
            def _():
                first.wait_send()


def spread(piece, count, lanes, wide, tall):
    depth = piece.shape[1]
    steps = count // 2
    dma = pltpu.SemaphoreType.DMA
    return pl.pallas_call(
        functools.partial(spread_kernel, count, lanes, wide, tall),
        out_shape=jax.ShapeDtypeStruct((count, wide + tall, depth), jnp.float32),
        in_specs=[pl.BlockSpec(memory_space=pl.ANY)],
        out_specs=pl.BlockSpec(memory_space=pl.ANY),
        scratch_shapes=[
            dma, dma((steps,)), dma((steps,)), dma((steps,)), dma((steps,)), dma((count,)), dma((count,)), dma((count,)),
        ],
        compiler_params=pltpu.CompilerParams(collective_id=0, has_side_effects=True),
    )(piece)


def filter_kernel(data_ref, weight_ref, high_ref, low_ref):
    count, _, depth = data_ref.shape
    weight_high, weight_low = split(weight_ref[...])

    def product(left, right):
        return jnp.dot(left, right, preferred_element_type=jnp.float32)

    before = None
    for group in range(count):
        now = split(data_ref[group])
        if before is None:
            ext_high, ext_low = now
            use_high, use_low = weight_high[depth:], weight_low[depth:]
        else:
            ext_high = jnp.concatenate([before[0], now[0]], axis=1)
            ext_low = jnp.concatenate([before[1], now[1]], axis=1)
            use_high, use_low = weight_high, weight_low
        value = product(ext_high, use_high) + (product(ext_high, use_low) + product(ext_low, use_high))
        high, low = split(value)
        high_ref[:, group * depth : (group + 1) * depth] = high
        low_ref[:, group * depth : (group + 1) * depth] = low
        before = now


def filter_all(data, weight):
    count, total, depth = data.shape
    tile = tile_of(total, 512)
    out = jax.ShapeDtypeStruct((total, count * depth), jnp.bfloat16)
    spec = pl.BlockSpec((tile, count * depth), lambda i: (i, 0))
    return pl.pallas_call(
        filter_kernel,
        grid=(total // tile,),
        in_specs=[
            pl.BlockSpec((count, tile, depth), lambda i: (0, i, 0)),
            pl.BlockSpec(weight.shape, lambda i: (0, 0)),
        ],
        out_specs=[spec, spec],
        out_shape=[out, out],
        compiler_params=pltpu.CompilerParams(vmem_limit_bytes=VMEM_LIMIT),
    )(data, weight)


def gram_kernel(start_ref, ah_ref, al_ref, bh_ref, bl_ref, normal_ref, out_ref):
    tall, wide = out_ref.shape
    row = start_ref[0] + pl.program_id(0) * tall
    col = start_ref[1] + pl.program_id(1) * wide
    some = row + tall - 1 >= col
    full = row >= col + wide - 1

    def gram():
        def product(left, right):
            return lax.dot_general(left, right, (((1,), (1,)), ((), ())), preferred_element_type=jnp.float32)

        high = ah_ref[...]
        return product(high, bh_ref[...]) + (product(high, bl_ref[...]) + product(al_ref[...], bh_ref[...]))

    @pl.when(full)
    def _():
        out_ref[...] = normal_ref[...] + gram()

    @pl.when(some & jnp.logical_not(full))
    def _():
        rows = row + lax.broadcasted_iota(jnp.int32, (tall, wide), 0)
        cols = col + lax.broadcasted_iota(jnp.int32, (tall, wide), 1)
        out_ref[...] = normal_ref[...] + jnp.where(rows >= cols, gram(), 0.0)

    @pl.when(jnp.logical_not(some))
    def _():
        out_ref[...] = normal_ref[...]


def gram_add(start, high, low, normal_in, wide_total):
    tall_total = normal_in.shape[0]
    deep = high.shape[1]
    tall, wide = tile_of(tall_total, 1024), tile_of(wide_total, 512)
    skip = wide_total // tall
    left = pl.BlockSpec((tall, deep), lambda i, j, s: (skip + i, 0))
    right = pl.BlockSpec((wide, deep), lambda i, j, s: (j, 0))
    tile = pl.BlockSpec((tall, wide), lambda i, j, s: (i, j))
    return pl.pallas_call(
        gram_kernel,
        grid_spec=pltpu.PrefetchScalarGridSpec(
            num_scalar_prefetch=1,
            grid=(tall_total // tall, wide_total // wide),
            in_specs=[left, left, right, right, tile],
            out_specs=tile,
        ),
        out_shape=jax.ShapeDtypeStruct(normal_in.shape, jnp.float32),
        compiler_params=pltpu.CompilerParams(vmem_limit_bytes=VMEM_LIMIT),
    )(start, high, low, high, low, normal_in)


def body(design, taps, order, normal_in):
    depth = design.shape[0]
    count, lanes = lax.axis_size("tr"), lax.axis_size("tc")
    tall, wide = normal_in.shape
    row, col = lax.axis_index("tr"), lax.axis_index("tc")
    everything = lax.all_gather(design.T, "tc", axis=0, tiled=True)
    piece = permute_rows(everything, lax.dynamic_slice_in_dim(order, col * wide, wide, 0))
    data = spread(piece, count, lanes, wide, tall)
    high, low = filter_all(data, toeplitz_of(taps, depth))
    start = jnp.stack([row * tall, col * wide]).astype(jnp.int32)
    return gram_add(start, high, low, normal_in, wide)


def solution(mesh):
    return jax.shard_map(
        body,
        mesh=mesh,
        in_specs=(P("tr", "tc"), P(), P(), P("tr", "tc")),
        out_specs=P("tr", "tc"),
        check_vma=False,
    )
```

time: 878 us -> 496 us (0.56)
  the two profiles are of different devices: /device:TPU:24 before, /device:TPU:11 now
where the time goes in v1:
time: 496 us
  Pallas kernels  419 us (84%)
  waiting for transfers between devices  56.1 us (11%)
  between operations  13.5 us (3%)
  local copies, waits for them, and re-layouts  5.52 us (1%)
    pallas_call x1, Pallas kernels, spread(): pl.pallas_call(functools.partial(spread_kernel, count, lanes, wide, tall)...  320 us
    pallas_call x1, Pallas kernels, gram_add(): pl.pallas_call(gram_kernel, grid_spec=pltpu.PrefetchScalarGridSpec(num_sc...  61.5 us
    all_gather x1, waiting for transfers between devices, body(): everything = lax.all_gather(design.T, 'tc', axis=0, tiled=True)  56.1 us
    pallas_call x1, Pallas kernels, filter_all(): pl.pallas_call(filter_kernel, grid=(total // tile,), in_specs=[pl.BlockSp...  27.4 us
    pallas_call x1, Pallas kernels, permute_rows(): pl.pallas_call(permute_kernel, grid_spec=pltpu.PrefetchScalarGridSpec(num...  10.1 us
  transfers between devices with their start and end apart: 1, of which 1 were waited for; matrix products, arithmetic and copies ran while one was open for 1% of the time, Pallas kernels for 0%

profile of v1, /device:TPU:11, one launch (start us, length us, event | category | flops | bytes accessed | tf_op | source)
XLA Modules:
  0.0 495.6 jit_solution(16741259491769968864)
XLA Ops:
  6.5 0.0 all-gather.2.cloned.1.call-start
  6.5 2.9 copy.6
  9.4 0.0 all-gather.2.cloned.1.call-update
  9.5 0.7 pad_maximum_fusion
  10.1 0.1 tile.4
  10.2 0.5 tile.10
  10.7 0.1 reshape.4
  10.8 0.7 slice.9.weight_ref
  11.5 1.3 dynamic_slice.3.order_ref
  12.8 0.6 pad_add_fusion.start_ref
  13.4 56.1 %all-gather.2.cloned.1.call-done.src_ref = f32[16384,128]{1,0:T(8,128)} async-done(((f32[4096,128]{1,0:T(8,128)}), f32[16384,128]{1,0:T(8,128)}) %all-gather.2.cloned.1.call-update) | async-done | bytes 8388624 | tf_op jit(solution)/shard_map/all_gather | solution.py:313
  69.4 10.1 %shard_map.46.piece_ref = f32[4096,128]{1,0:T(8,128)} custom-call(s32[4096]{0:T(1024)} %dynamic_slice.3.order_ref, f32[16384,128]{1,0:T(8,128)} %all-gather.2.cloned.1.call-done.src_ref), custom_call_target="tpu_custom_call" | custom-call | tf_op jit(solution)/shard_map/pallas_call | solution.py:48
  79.5 320.3 %shard_map.47.data_ref = f32[8,6144,128]{2,1,0:T(8,128)} custom-call(f32[4096,128]{1,0:T(8,128)} %shard_map.46.piece_ref), custom_call_target="tpu_custom_call" | custom-call | tf_op jit(solution)/shard_map/pallas_call | solution.py:204
  399.8 27.4 %shard_map.48 = (bf16[6144,1024]{1,0:T(8,128)(2,1)}, bf16[6144,1024]{1,0:T(8,128)(2,1)}) custom-call(f32[8,6144,128]{2,1,0:T(8,128)} %shard_map.47.data_ref, f32[256,128]{1,0:T(8,128)} %slice.9.weight_ref), custom_call_target="tpu_custom_call" | custom-call | tf_op jit(solution)/shard_map/pallas_call | solution.py:245
  427.2 61.5 %shard_map.49 = f32[2048,4096]{1,0:T(8,128)} custom-call(s32[2]{0:T(128)} %pad_add_fusion.start_ref, bf16[6144,1024]{1,0:T(8,128)(2,1)} %get-tuple-element.7.ah_ref.bh_ref, bf16[6144,1024]{1,0:T(8,128)(2,1)} %get-tuple-element.8.al_ref.bl_ref, bf16[6144,1024]{1,0:T(8,128)(2,1)} %get-tuple-element.7.ah_ref.bh_ref, ...), custom_call_target="tpu_custom_call" | custom-call | tf_op jit(solution)/shard_map/pallas_call | solution.py:295
  (3 shorter events, 0.0 us)
Async XLA Ops:
  6.5 62.9 %all-gather.2.cloned.1.call-start = ((), (), s32[]{:S(2)}) async-start(), calls=%async_computation | async-start | bytes 10485760 | tf_op jit(solution)/shard_map/all_gather | solution.py:313
Sparse Core Ops, SparseCore 0:
  9.6 59.8 all-gather.1

commit v2 on v1

--- a/solution.py
+++ b/solution.py
@@ -75,7 +75,7 @@
     return jnp.where(place < count // 2, 2 * place, 2 * (count - 1 - place) + 1)
 
 
-def spread_kernel(count, lanes, wide, tall, piece_ref, out_ref, own_sem, rs_sem, rr_sem, ls_sem, lr_sem, cs_sem, cr_sem, fill_sem):
+def spread_kernel(count, lanes, wide, tall, piece_ref, out_ref, own_sem, rs_sem, rr_sem, ls_sem, lr_sem, cs_sem, cr_sem):
     row = lax.axis_index("tr")
     col = lax.axis_index("tc")
     place = ring_place(row, count)
@@ -136,8 +136,7 @@
             src_ref=target, dst_ref=target, send_sem=cs_sem.at[turn], recv_sem=cr_sem.at[turn],
             device_id=(row, col - 1), device_id_type=MESH,
         )
-        fill = pltpu.make_async_copy(source, target, fill_sem.at[turn])
-        return first, relay, fill
+        return first, relay
 
     offsets = [[0]] + [[-s, s] for s in range(1, steps)] + [[steps]]
     turns = []
@@ -146,11 +145,7 @@
 
     def chain_owner(level):
         for turn, off in turns[level]:
-            first, _, fill = chain(turn, ring_member(place + off, count), level == 0)
-
-            @pl.when(col == owner)
-            def _():
-                fill.start()
+            first, _ = chain(turn, ring_member(place + off, count), level == 0)
 
             @pl.when((col == owner) & (col > 0))
             def _():
@@ -158,7 +153,7 @@
 
     def chain_relay(level):
         for turn, off in turns[level]:
-            _, relay, _ = chain(turn, ring_member(place + off, count), level == 0)
+            _, relay = chain(turn, ring_member(place + off, count), level == 0)
 
             @pl.when(col < owner)
             def _():
@@ -172,12 +167,10 @@
         ring(step, 1).start()
         ring(step, -1).start()
         chain_owner(step)
-        if step >= 1:
-            chain_relay(step - 1)
+        chain_relay(step)
         ring(step, 1).wait_recv()
         ring(step, -1).wait_recv()
     chain_owner(steps)
-    chain_relay(steps - 1)
     chain_relay(steps)
 
     own.wait()
@@ -186,11 +179,7 @@
         ring(step, -1).wait_send()
     for level in range(steps + 1):
         for turn, off in turns[level]:
-            first, _, fill = chain(turn, ring_member(place + off, count), level == 0)
-
-            @pl.when(col == owner)
-            def _():
-                fill.wait()
+            first, _ = chain(turn, ring_member(place + off, count), level == 0)
 
             @pl.when((col <= owner) & (col > 0))
             def _():
@@ -207,7 +196,7 @@
         in_specs=[pl.BlockSpec(memory_space=pl.ANY)],
         out_specs=pl.BlockSpec(memory_space=pl.ANY),
         scratch_shapes=[
-            dma, dma((steps,)), dma((steps,)), dma((steps,)), dma((steps,)), dma((count,)), dma((count,)), dma((count,)),
+            dma, dma((steps,)), dma((steps,)), dma((steps,)), dma((steps,)), dma((count,)), dma((count,)),
         ],
         compiler_params=pltpu.CompilerParams(collective_id=0, has_side_effects=True),
     )(piece)
@@ -230,7 +219,8 @@
             ext_high = jnp.concatenate([before[0], now[0]], axis=1)
             ext_low = jnp.concatenate([before[1], now[1]], axis=1)
             use_high, use_low = weight_high, weight_low
-        value = product(ext_high, use_high) + (product(ext_high, use_low) + product(ext_low, use_high))
+        both = product(ext_high, jnp.concatenate([use_high, use_low], axis=1))
+        value = both[:, :depth] + (both[:, depth:] + product(ext_low, use_high))
         high, low = split(value)
         high_ref[:, group * depth : (group + 1) * depth] = high
         low_ref[:, group * depth : (group + 1) * depth] = low
@@ -288,8 +278,7 @@
     tall_total = normal_in.shape[0]
     deep = high.shape[1]
     tall, wide = tile_of(tall_total, 1024), tile_of(wide_total, 512)
-    skip = wide_total // tall
-    left = pl.BlockSpec((tall, deep), lambda i, j, s: (skip + i, 0))
+    left = pl.BlockSpec((tall, deep), lambda i, j, s: (s[2] // tall + i, 0))
     right = pl.BlockSpec((wide, deep), lambda i, j, s: (j, 0))
     tile = pl.BlockSpec((tall, wide), lambda i, j, s: (i, j))
     return pl.pallas_call(
@@ -314,7 +303,8 @@
     piece = permute_rows(everything, lax.dynamic_slice_in_dim(order, col * wide, wide, 0))
     data = spread(piece, count, lanes, wide, tall)
     high, low = filter_all(data, toeplitz_of(taps, depth))
-    start = jnp.stack([row * tall, col * wide]).astype(jnp.int32)
+    inside = jnp.where(lax.div(row * tall, wide) == col, lax.rem(row * tall, wide), wide)
+    start = jnp.stack([row * tall, col * wide, inside]).astype(jnp.int32)
     return gram_add(start, high, low, normal_in, wide)
 
 

time: 496 us -> 355 us (0.72)
  the two profiles are of different devices: /device:TPU:11 before, /device:TPU:24 now
where the time goes in v2:
time: 355 us; the launch traced here: 354 us
  Pallas kernels  278 us (78%)
  waiting for transfers between devices  55.5 us (16%)
  between operations  13.5 us (4%)
  local copies, waits for them, and re-layouts  5.52 us (2%)
    pallas_call x1, Pallas kernels, spread(): pl.pallas_call(functools.partial(spread_kernel, count, lanes, wide, tall)...  180 us
    pallas_call x1, Pallas kernels, gram_add(): pl.pallas_call(gram_kernel, grid_spec=pltpu.PrefetchScalarGridSpec(num_sc...  62.4 us
    all_gather x1, waiting for transfers between devices, body(): everything = lax.all_gather(design.T, 'tc', axis=0, tiled=True)  55.5 us
    pallas_call x1, Pallas kernels, filter_all(): pl.pallas_call(filter_kernel, grid=(total // tile,), in_specs=[pl.BlockSp...  25.1 us
    pallas_call x1, Pallas kernels, permute_rows(): pl.pallas_call(permute_kernel, grid_spec=pltpu.PrefetchScalarGridSpec(num...  10.1 us
  transfers between devices with their start and end apart: 1, of which 1 were waited for; matrix products, arithmetic and copies ran while one was open for 1% of the time, Pallas kernels for 0%

profile of v2, /device:TPU:24, one launch (start us, length us, event | category | flops | bytes accessed | tf_op | source)
XLA Modules:
  0.0 353.6 jit_solution(6786133846783327501)
XLA Ops:
  6.5 0.0 all-gather.2.cloned.1.call-start
  6.5 2.9 copy.6
  9.4 0.0 all-gather.2.cloned.1.call-update
  9.5 0.7 pad_maximum_fusion
  10.1 0.1 tile.4
  10.2 0.5 tile.10
  10.7 0.1 reshape.4
  10.8 0.7 slice.9.weight_ref
  11.5 1.3 dynamic_slice.3.order_ref
  12.8 0.6 pad_add_fusion.start_ref
  13.4 55.5 %all-gather.2.cloned.1.call-done.src_ref = f32[16384,128]{1,0:T(8,128)} async-done(((f32[4096,128]{1,0:T(8,128)}), f32[16384,128]{1,0:T(8,128)}) %all-gather.2.cloned.1.call-update) | async-done | bytes 8388624 | tf_op jit(solution)/shard_map/all_gather | solution.py:302
  68.9 10.1 %shard_map.46.piece_ref = f32[4096,128]{1,0:T(8,128)} custom-call(s32[4096]{0:T(1024)} %dynamic_slice.3.order_ref, f32[16384,128]{1,0:T(8,128)} %all-gather.2.cloned.1.call-done.src_ref), custom_call_target="tpu_custom_call" | custom-call | tf_op jit(solution)/shard_map/pallas_call | solution.py:48
  78.9 180.3 %shard_map.47.data_ref = f32[8,6144,128]{2,1,0:T(8,128)} custom-call(f32[4096,128]{1,0:T(8,128)} %shard_map.46.piece_ref), custom_call_target="tpu_custom_call" | custom-call | tf_op jit(solution)/shard_map/pallas_call | solution.py:193
  259.2 25.1 %shard_map.48 = (bf16[6144,1024]{1,0:T(8,128)(2,1)}, bf16[6144,1024]{1,0:T(8,128)(2,1)}) custom-call(f32[8,6144,128]{2,1,0:T(8,128)} %shard_map.47.data_ref, f32[256,128]{1,0:T(8,128)} %slice.9.weight_ref), custom_call_target="tpu_custom_call" | custom-call | tf_op jit(solution)/shard_map/pallas_call | solution.py:235
  284.3 62.4 %shard_map.49 = f32[2048,4096]{1,0:T(8,128)} custom-call(s32[3]{0:T(128)} %pad_add_fusion.start_ref, bf16[6144,1024]{1,0:T(8,128)(2,1)} %get-tuple-element.7.ah_ref.bh_ref, bf16[6144,1024]{1,0:T(8,128)(2,1)} %get-tuple-element.8.al_ref.bl_ref, bf16[6144,1024]{1,0:T(8,128)(2,1)} %get-tuple-element.7.ah_ref.bh_ref, ...), custom_call_target="tpu_custom_call" | custom-call | tf_op jit(solution)/shard_map/pallas_call | solution.py:284
  (3 shorter events, 0.0 us)
Async XLA Ops:
  6.5 62.3 %all-gather.2.cloned.1.call-start = ((), (), s32[]{:S(2)}) async-start(), calls=%async_computation | async-start | bytes 10485760 | tf_op jit(solution)/shard_map/all_gather | solution.py:302
Sparse Core Ops, SparseCore 0:
  9.6 59.2 all-gather.1

commit v3 on v2

--- a/solution.py
+++ b/solution.py
@@ -75,7 +75,10 @@
     return jnp.where(place < count // 2, 2 * place, 2 * (count - 1 - place) + 1)
 
 
-def spread_kernel(count, lanes, wide, tall, piece_ref, out_ref, own_sem, rs_sem, rr_sem, ls_sem, lr_sem, cs_sem, cr_sem):
+def spread_kernel(
+    count, lanes, wide, tall, piece_ref, weight_ref, high_ref, low_ref, out_ref, high_buf, low_buf,
+    own_sem, rs_sem, rr_sem, ls_sem, lr_sem, cs_sem, cr_sem, high_sem, low_sem,
+):
     row = lax.axis_index("tr")
     col = lax.axis_index("tc")
     place = ring_place(row, count)
@@ -163,17 +166,83 @@
             def _():
                 relay.start()
 
+    depth = piece_ref.shape[1]
+    weight_high, weight_low = split(weight_ref[...])
+    weight_both = jnp.concatenate([weight_high, weight_low], axis=1)
+
+    def product(a, b):
+        return jnp.dot(a, b, preferred_element_type=jnp.float32)
+
+    def away(group):
+        gap = lax.rem(ring_place(group, count) - place + count, count)
+        return jnp.minimum(gap, count - gap)
+
+    def ready(group):
+        return jnp.maximum(away(group), away(jnp.maximum(group - 1, 0)))
+
+    def flush(part, group, begin, size):
+        rows = pl.ds(begin, size)
+        lanes_of = pl.ds(pl.multiple_of(group * depth, depth), depth)
+        return [
+            pltpu.make_async_copy(buf.at[group, rows], ref.at[rows, lanes_of], sem.at[part, group])
+            for buf, ref, sem in ((high_buf, high_ref, high_sem), (low_buf, low_ref, low_sem))
+        ]
+
+    def filter_part(level, part, begin, size):
+        tile = tile_of(size, 256)
+
+        def one(group, carry):
+            @pl.when(ready(group) == level)
+            def _():
+                def rows_of(index, inner):
+                    rows = pl.ds(pl.multiple_of(begin + index * tile, tile), tile)
+                    old = jnp.where(group > 0, out_ref[jnp.maximum(group - 1, 0), rows, :], 0.0)
+                    old_high, old_low = split(old)
+                    new_high, new_low = split(out_ref[group, rows, :])
+                    both = product(jnp.concatenate([old_high, new_high], axis=1), weight_both)
+                    rest = product(jnp.concatenate([old_low, new_low], axis=1), weight_high)
+                    high, low = split(both[:, :depth] + (both[:, depth:] + rest))
+                    high_buf[group, rows, :] = high
+                    low_buf[group, rows, :] = low
+                    return inner
+
+                lax.fori_loop(0, size // tile, rows_of, 0)
+                for copy in flush(part, group, begin, size):
+                    copy.start()
+
+            return carry
+
+        lax.fori_loop(0, count, one, 0)
+
+    def work(level):
+        chain_owner(level)
+        filter_part(level, 0, 0, wide)
+        chain_relay(level)
+
+        @pl.when(col < owner)
+        def _():
+            filter_part(level, 1, wide, tall)
+
     for step in range(steps):
         ring(step, 1).start()
         ring(step, -1).start()
-        chain_owner(step)
-        chain_relay(step)
+        if step == 0:
+            own.wait()
+        work(step)
         ring(step, 1).wait_recv()
         ring(step, -1).wait_recv()
-    chain_owner(steps)
-    chain_relay(steps)
-
-    own.wait()
+    work(steps)
+
+    for group in range(count):
+        for copy in flush(0, group, 0, wide):
+            copy.wait()
+
+    @pl.when(col < owner)
+    def _():
+        for group in range(count):
+            for copy in flush(1, group, wide, tall):
+                copy.wait()
+
     for step in range(steps):
         ring(step, 1).wait_send()
         ring(step, -1).wait_send()
@@ -186,63 +255,26 @@
                 first.wait_send()
 
 
-def spread(piece, count, lanes, wide, tall):
+def spread(piece, weight, count, lanes, wide, tall):
     depth = piece.shape[1]
     steps = count // 2
     dma = pltpu.SemaphoreType.DMA
+    out = jax.ShapeDtypeStruct((wide + tall, count * depth), jnp.bfloat16)
+    hold = (count, wide + tall, depth)
     return pl.pallas_call(
         functools.partial(spread_kernel, count, lanes, wide, tall),
-        out_shape=jax.ShapeDtypeStruct((count, wide + tall, depth), jnp.float32),
-        in_specs=[pl.BlockSpec(memory_space=pl.ANY)],
-        out_specs=pl.BlockSpec(memory_space=pl.ANY),
+        out_shape=[out, out],
+        in_specs=[pl.BlockSpec(memory_space=pl.ANY), pl.BlockSpec(memory_space=pltpu.VMEM)],
+        out_specs=[pl.BlockSpec(memory_space=pl.ANY)] * 2,
         scratch_shapes=[
+            pltpu.VMEM(hold, jnp.float32), pltpu.VMEM(hold, jnp.bfloat16), pltpu.VMEM(hold, jnp.bfloat16),
             dma, dma((steps,)), dma((steps,)), dma((steps,)), dma((steps,)), dma((count,)), dma((count,)),
+            dma((2, count)), dma((2, count)),
         ],
-        compiler_params=pltpu.CompilerParams(collective_id=0, has_side_effects=True),
-    )(piece)
-
-
-def filter_kernel(data_ref, weight_ref, high_ref, low_ref):
-    count, _, depth = data_ref.shape
-    weight_high, weight_low = split(weight_ref[...])
-
-    def product(left, right):
-        return jnp.dot(left, right, preferred_element_type=jnp.float32)
-
-    before = None
-    for group in range(count):
-        now = split(data_ref[group])
-        if before is None:
-            ext_high, ext_low = now
-            use_high, use_low = weight_high[depth:], weight_low[depth:]
-        else:
-            ext_high = jnp.concatenate([before[0], now[0]], axis=1)
-            ext_low = jnp.concatenate([before[1], now[1]], axis=1)
-            use_high, use_low = weight_high, weight_low
-        both = product(ext_high, jnp.concatenate([use_high, use_low], axis=1))
-        value = both[:, :depth] + (both[:, depth:] + product(ext_low, use_high))
-        high, low = split(value)
-        high_ref[:, group * depth : (group + 1) * depth] = high
-        low_ref[:, group * depth : (group + 1) * depth] = low
-        before = now
-
-
-def filter_all(data, weight):
-    count, total, depth = data.shape
-    tile = tile_of(total, 512)
-    out = jax.ShapeDtypeStruct((total, count * depth), jnp.bfloat16)
-    spec = pl.BlockSpec((tile, count * depth), lambda i: (i, 0))
-    return pl.pallas_call(
-        filter_kernel,
-        grid=(total // tile,),
-        in_specs=[
-            pl.BlockSpec((count, tile, depth), lambda i: (0, i, 0)),
-            pl.BlockSpec(weight.shape, lambda i: (0, 0)),
-        ],
-        out_specs=[spec, spec],
-        out_shape=[out, out],
-        compiler_params=pltpu.CompilerParams(vmem_limit_bytes=VMEM_LIMIT),
-    )(data, weight)
+        compiler_params=pltpu.CompilerParams(
+            collective_id=0, has_side_effects=True, vmem_limit_bytes=VMEM_LIMIT
+        ),
+    )(piece, weight)
 
 
 def gram_kernel(start_ref, ah_ref, al_ref, bh_ref, bl_ref, normal_ref, out_ref):
@@ -301,8 +333,7 @@
     row, col = lax.axis_index("tr"), lax.axis_index("tc")
     everything = lax.all_gather(design.T, "tc", axis=0, tiled=True)
     piece = permute_rows(everything, lax.dynamic_slice_in_dim(order, col * wide, wide, 0))
-    data = spread(piece, count, lanes, wide, tall)
-    high, low = filter_all(data, toeplitz_of(taps, depth))
+    high, low = spread(piece, toeplitz_of(taps, depth), count, lanes, wide, tall)
     inside = jnp.where(lax.div(row * tall, wide) == col, lax.rem(row * tall, wide), wide)
     start = jnp.stack([row * tall, col * wide, inside]).astype(jnp.int32)
     return gram_add(start, high, low, normal_in, wide)

time: 355 us -> 346 us (0.975)
  Pallas kernels: 278 us -> 270 us
    pallas_call x1 -> x0, Pallas kernels: 25.1 us -> none  [filter_all(): pl.pallas_call(filter_kernel, grid=(total // tile,), in_specs=[pl.BlockSp...]
    pallas_call x1, Pallas kernels: 180 us -> 197 us  [spread(): pl.pallas_call(functools.partial(spread_kernel, count, lanes, wide, tall)...]
where the time goes in v3:
time: 346 us
  Pallas kernels  270 us (78%)
  waiting for transfers between devices  55.4 us (16%)
  between operations  13.5 us (4%)
  local copies, waits for them, and re-layouts  5.51 us (2%)
    pallas_call x1, Pallas kernels, spread(): pl.pallas_call(functools.partial(spread_kernel, count, lanes, wide, tall)...  197 us
    pallas_call x1, Pallas kernels, gram_add(): pl.pallas_call(gram_kernel, grid_spec=pltpu.PrefetchScalarGridSpec(num_sc...  62.5 us
    all_gather x1, waiting for transfers between devices, body(): everything = lax.all_gather(design.T, 'tc', axis=0, tiled=True)  55.4 us
    pallas_call x1, Pallas kernels, permute_rows(): pl.pallas_call(permute_kernel, grid_spec=pltpu.PrefetchScalarGridSpec(num...  10.1 us
  transfers between devices with their start and end apart: 1, of which 1 were waited for; matrix products, arithmetic and copies ran while one was open for 1% of the time, Pallas kernels for 0%

profile of v3, /device:TPU:24, one launch (start us, length us, event | category | flops | bytes accessed | tf_op | source)
XLA Modules:
  0.0 345.6 jit_solution(15167865461659195147)
XLA Ops:
  6.5 0.0 all-gather.2.cloned.1.call-start
  6.5 2.9 copy.6
  9.4 0.0 all-gather.2.cloned.1.call-update
  9.5 0.7 pad_maximum_fusion
  10.1 0.1 tile.4
  10.2 0.5 tile.10
  10.7 0.1 reshape.4
  10.8 0.7 slice.9.weight_ref
  11.5 1.3 dynamic_slice.3.order_ref
  12.8 0.7 pad_add_fusion.start_ref
  13.5 55.4 %all-gather.2.cloned.1.call-done.src_ref = f32[16384,128]{1,0:T(8,128)} async-done(((f32[4096,128]{1,0:T(8,128)}), f32[16384,128]{1,0:T(8,128)}) %all-gather.2.cloned.1.call-update) | async-done | bytes 8388624 | tf_op jit(solution)/shard_map/all_gather | solution.py:334
  68.9 10.1 %shard_map.46.piece_ref = f32[4096,128]{1,0:T(8,128)} custom-call(s32[4096]{0:T(1024)} %dynamic_slice.3.order_ref, f32[16384,128]{1,0:T(8,128)} %all-gather.2.cloned.1.call-done.src_ref), custom_call_target="tpu_custom_call" | custom-call | tf_op jit(solution)/shard_map/pallas_call | solution.py:48
  78.9 197.3 %shard_map.47 = (bf16[6144,1024]{1,0:T(8,128)(2,1)}, bf16[6144,1024]{1,0:T(8,128)(2,1)}) custom-call(f32[4096,128]{1,0:T(8,128)} %shard_map.46.piece_ref, f32[256,128]{1,0:T(8,128)} %slice.9.weight_ref), custom_call_target="tpu_custom_call" | custom-call | tf_op jit(solution)/shard_map/pallas_call | solution.py:264
  276.3 62.5 %shard_map.48 = f32[2048,4096]{1,0:T(8,128)} custom-call(s32[3]{0:T(128)} %pad_add_fusion.start_ref, bf16[6144,1024]{1,0:T(8,128)(2,1)} %get-tuple-element.7.ah_ref.bh_ref, bf16[6144,1024]{1,0:T(8,128)(2,1)} %get-tuple-element.8.al_ref.bl_ref, bf16[6144,1024]{1,0:T(8,128)(2,1)} %get-tuple-element.7.ah_ref.bh_ref, ...), custom_call_target="tpu_custom_call" | custom-call | tf_op jit(solution)/shard_map/pallas_call | solution.py:316
  (3 shorter events, 0.0 us)
Async XLA Ops:
  6.5 62.3 %all-gather.2.cloned.1.call-start = ((), (), s32[]{:S(2)}) async-start(), calls=%async_computation | async-start | bytes 10485760 | tf_op jit(solution)/shard_map/all_gather | solution.py:334
Sparse Core Ops, SparseCore 0:
  9.6 59.2 all-gather.1
